TPU v7x, 32 devices: a whole 2x2x4 slice. The times are simulated.
32 devices in a mesh: lon: 16 (over z, y, x), lat: 2 (over core).
Axes of the slice: x: 2, y: 2, z: 4, core: 2. Of those that a mesh axis runs over, the one named last changes fastest.
Arguments:
- thermal_anomaly: float32 [16, 128, 256], P(None, 'lon', 'lat'), may hold values from -6 to 6
- saltiness_anomaly: float32 [16, 128, 256], P(None, 'lon', 'lat'), may hold values from -6 to 6
- zonal_current: float32 [16, 128, 256], P(None, 'lon', 'lat'), may hold values from -3 to 3
- meridional_current: float32 [16, 128, 256], P(None, 'lon', 'lat'), may hold values from -3 to 3
- bottom_ocean_layer: int32 [128, 256], P('lon', 'lat'), may hold values from 0 to 16
- seam_axis_meridian: int32 [1], replicated, may hold values from 0 to 255
- interface_diffusivity: float32 [15, 128, 256], P(None, 'lon', 'lat'), may hold values from 0.1 to 10
- atmospheric_forcing: float32 [2, 128, 256], P(None, 'lon', 'lat'), may hold values from -6 to 6
Outputs:
- temperature_next: float32 [16, 128, 256], P(None, 'lon', 'lat')
- salinity_next: float32 [16, 128, 256], P(None, 'lon', 'lat')
- zonal_next: float32 [16, 128, 256], P(None, 'lon', 'lat')
- meridional_next: float32 [16, 128, 256], P(None, 'lon', 'lat')
Inputs may be any that keep to these rules, and one draw needn't show every extreme that they name: `seam_axis_meridian`: an even code folds about a cell centre, an odd one about a cell corner.
All inputs are finite; a program needn't handle non-finite values.
Results may differ from a plain program's by a relative error of at most 0.0003.
Values sent between devices are 32-bit elements; how exact they have to be, the bound alone decides.
No kernel may reach another device: no remote copies, remote signals or barrier semaphores. Data moves between devices by JAX's collectives and lax.ppermute only.
A program may use at most 64 MiB of HBM per device.

v0:
```python
import functools

import jax
import jax.numpy as jnp
from jax import lax
from jax.experimental import pallas as pl
from jax.experimental.pallas import tpu as pltpu
from jax.sharding import PartitionSpec as P

TIME_STEP = 0.2
TRACER_DIFF = 0.2
MOMENTUM_VISC = 0.2
THERMAL_EXPANSION = 0.5
HALINE_CONTRACTION = 0.4
WIND_GAIN = 2.0
VERTICAL_VISC = 1.0

VMEM = pl.BlockSpec(memory_space=pltpu.VMEM)
SMEM = pl.BlockSpec(memory_space=pltpu.SMEM)
SUB = 8
SMALL = pltpu.CompilerParams(vmem_limit_bytes=4 * 2**20)
FIRST = pltpu.CompilerParams(vmem_limit_bytes=4 * 2**20)
LARGE = pltpu.CompilerParams(vmem_limit_bytes=8 * 2**20)


def lane_of(lanes):
    return lax.broadcasted_iota(jnp.int32, (SUB, lanes), 1)


def row_of(lanes):
    return lax.broadcasted_iota(jnp.int32, (SUB, lanes), 0)


def tall(value):
    missing = SUB - value.shape[0]
    if missing == 0:
        return value
    return jnp.concatenate([value, jnp.zeros((missing, value.shape[1]), value.dtype)], axis=0)


def edges_kernel(t_ref, s_ref, u_ref, v_ref, depth_ref, stress_ref, *outs):
    top_ref, bottom_ref, east_ref, west_ref, count_ref, wind_ref, first_ref = outs[:7]
    levels, width, lanes = t_ref.shape
    count_ref[...] = depth_ref[...].astype(jnp.float32)
    wind_ref[...] = stress_ref[...]
    even = lax.rem(lax.axis_index("lat"), 2) == 0
    lane = lane_of(lanes)
    for message, near, far in ((east_ref, width - 1, width - 2), (west_ref, 0, 1)):
        for place, field, column in (
            (0, t_ref, near),
            (1, t_ref, far),
            (2, s_ref, near),
            (3, s_ref, far),
            (4, u_ref, near),
            (5, v_ref, near),
        ):
            message[pl.ds(place * levels, levels), :] = field[:, column, :]
        depth = depth_ref[...].astype(jnp.float32)
        message[pl.ds(6 * levels, 8), :] = jnp.concatenate(
            [depth[near : near + 1], depth[far : far + 1]] * 4, axis=0
        )

    tops, bottoms = [], []
    for first, second, count in ((t_ref, s_ref, depth_ref), (u_ref, v_ref, None)):
        top = jnp.zeros((SUB, lanes), jnp.float32)
        bottom = jnp.zeros((SUB, lanes), jnp.float32)
        places = [(3 * k, first, k) for k in range(levels)]
        places += [(3 * (levels + k), second, k) for k in range(levels)]
        if count is not None:
            places.append((6 * levels, count, None))
        for start, ref, k in places:
            value = depth_ref[...].astype(jnp.float32) if k is None else ref[k]
            value = tall(value)
            here = jnp.logical_and(lane >= start, lane < start + 3)
            top = jnp.where(here, pltpu.roll(value, start + 3, 1), top)
            bottom = jnp.where(here, pltpu.roll(value, start, 1), bottom)
        bottom = jnp.where(lax.rem(lane, 3) == 2, pltpu.roll(bottom, 2, 1), bottom)
        tops.append(top[:width])
        bottoms.append(bottom[:width])
    for index in range(2):
        rows = pl.ds(index * width, width)
        top_ref[rows, :] = tops[index]
        bottom_ref[rows, :] = bottoms[index]
        first_ref[rows, :] = jnp.where(even, tops[index], bottoms[index])
        first_ref[pl.ds((2 + index) * width, width), :] = tops[index]
        for second_ref in outs[7:]:
            second_ref[rows, :] = jnp.where(even, bottoms[index], tops[index])


def corners_kernel(top_ref, east_base_ref, west_base_ref, seam_ref, *refs):
    north_ref, south_ref, east_ref, fold_ref, west_ref, rest_ref = refs[-6:]
    received = refs[:-6]
    lanes = top_ref.shape[1]
    width = top_ref.shape[0] // 2
    lat = lax.axis_index("lat")
    even = lax.rem(lat, 2) == 0
    halo = pl.ds(0, 2 * width)
    from_first = received[0][halo, :]
    from_second = received[1][...] if len(received) > 1 else jnp.zeros_like(from_first)
    north = jnp.where(even, from_first, from_second)
    south = jnp.where(even, from_second, from_first)
    north_ref[...] = north
    south_ref[...] = south
    base = west_base_ref.shape[0] - 8
    near = width - 1
    east_ref[pl.ds(0, base), :] = east_base_ref[pl.ds(0, base), :]
    east_ref[pl.ds(base, 8), :] = jnp.concatenate(
        [
            east_base_ref[pl.ds(base, 2), :],
            north[near : near + 1],
            north[width + near : width + near + 1],
            jnp.zeros((4, lanes), jnp.float32),
        ],
        axis=0,
    )
    west_ref[pl.ds(0, base), :] = west_base_ref[pl.ds(0, base), :]
    west_ref[pl.ds(base, 8), :] = jnp.concatenate(
        [
            west_base_ref[pl.ds(base, 2), :],
            north[0:1],
            north[width : width + 1],
            south[0:1],
            south[width : width + 1],
            jnp.zeros((2, lanes), jnp.float32),
        ],
        axis=0,
    )
    is_top = lat == lax.axis_size("lat") - 1
    code = seam_ref[0]
    corner = lax.rem(code, 2) == 1
    for index in range(2):
        rows = pl.ds(index * width, width)
        theirs = received[0][pl.ds((2 + index) * width, width), :]
        top = tall(jnp.where(is_top, top_ref[rows, :], theirs))
        fold_ref[rows, :] = jnp.where(corner, top, pltpu.roll(top, 1, 1))[:width]
    unused = fold_ref.shape[0] - 2 * width
    fold_ref[pl.ds(2 * width, unused), :] = jnp.zeros((unused, lanes), jnp.float32)
    rest_ref[...] = jnp.full((SUB, lanes), lax.rem(code, width), jnp.int32)


def mixing_constants(levels):
    gain = TIME_STEP * VERTICAL_VISC
    inner, last, ratio = [], [], 0.0
    for k in range(levels):
        above = gain if k > 0 else 0.0
        last.append(1.0 / (1.0 + above + above * ratio))
        pivot = 1.0 + above + gain + above * ratio
        inner.append(1.0 / pivot)
        ratio = -gain / pivot
    return inner, last


def keep_kernel(message_ref, kept_ref):
    kept_ref[...] = message_ref[...]


def mirror_kernel(own_tiles, own_ref, rest_ref, *refs):
    tiles, (mirror_ref, tiles_ref) = refs[:-2], refs[-2:]
    width = tiles_ref.shape[1] // 3
    rest = rest_ref[0, 0]
    lon = lax.axis_index("lon")
    for index in range(2):
        half = pl.ds(index * width, width)
        for place, ref in enumerate(tiles):
            tile = ref[half, :]
            for device in own_tiles[place]:
                tile = jnp.where(lon == device, own_ref[half, :], tile)
            tiles_ref[index, pl.ds(place * width, width), :] = tile
        for i in range(-1, width + 1):
            mirror_ref[index, pl.ds(i + 1, 1), :] = tiles_ref[
                index, pl.ds(width + rest - i, 1), :
            ]


def step_kernel(
    t_ref,
    s_ref,
    u_ref,
    v_ref,
    depth_ref,
    mix_ref,
    wind_ref,
    bottom_ref,
    north_ref,
    south_ref,
    west_ref,
    east_ref,
    mirror_ref,
    t_out,
    s_out,
    u_out,
    v_out,
    gx_t_ref,
    gx_s_ref,
    u2_ref,
    v2_ref,
    val_ref,
    near_ref,
    far_ref,
):
    levels, width, lanes = t_ref.shape
    lat = lax.axis_index("lat")
    lat_count = lax.axis_size("lat")
    is_top = lat == lat_count - 1
    lane = lane_of(lanes)
    row = row_of(lanes)
    depth_at = 6 * levels
    count_at = 6 * levels + 2

    def half(ref, index):
        return tall(ref[pl.ds(index * width, width), :])

    north, north_uv = (
        jnp.where(
            is_top, sign * tall(mirror_ref[index, pl.ds(1, width), :]), half(north_ref, index)
        )
        for index, sign in ((0, 1.0), (1, -1.0))
    )
    south, south_uv = half(south_ref, 0), half(south_ref, 1)
    bottom = half(bottom_ref, 0)

    def line(ref, index):
        return jnp.broadcast_to(ref[pl.ds(index, 1), :], (SUB, lanes))

    def mirror_line(index, i):
        return jnp.broadcast_to(mirror_ref[index, pl.ds(i + 1, 1), :], (SUB, lanes))

    nw = jnp.where(is_top, mirror_line(0, -1), line(west_ref, depth_at + 2))
    nw_uv = jnp.where(is_top, -mirror_line(1, -1), line(west_ref, depth_at + 3))
    ne = jnp.where(is_top, mirror_line(0, width), line(east_ref, depth_at + 2))
    se = line(east_ref, depth_at + 4)
    se_uv = line(east_ref, depth_at + 5)

    def to_east(value, halo):
        return jnp.where(row == width - 1, halo, pltpu.roll(value, SUB - 1, 0))

    def to_west(value, halo):
        return jnp.where(row == 0, halo, pltpu.roll(value, 1, 0))

    def to_north(value, halo):
        return jnp.where(lane == lanes - 1, halo, pltpu.roll(value, lanes - 1, 1))

    def to_south(value, halo):
        return jnp.where(lane == 0, halo, pltpu.roll(value, 1, 1))

    def at_north(message, index):
        return pltpu.roll(message, lanes - 1 - index, 1)

    def at_south(message, index):
        return pltpu.roll(message, (lanes - index) % lanes, 1)

    depth = tall(depth_ref[...])
    d_n = to_north(depth, at_north(north, count_at))
    d_nn = to_north(d_n, at_north(north, count_at - 1))
    d_s = to_south(depth, at_south(south, count_at))
    d_e = to_east(depth, line(east_ref, depth_at))
    d_ee = to_east(d_e, line(east_ref, depth_at + 1))
    d_w = to_west(depth, line(west_ref, depth_at))
    east_line = line(east_ref, depth_at)
    west_line = line(west_ref, depth_at)
    d_ne = to_east(d_n, to_north(east_line, at_north(ne, count_at)))
    d_se = to_east(d_s, to_south(east_line, at_south(se, count_at)))
    d_nw = to_west(d_n, to_north(west_line, at_north(nw, count_at)))
    d_u = jnp.minimum(depth, d_e)
    d_v = jnp.minimum(depth, d_n)
    u_neighbours = [
        jnp.minimum(d_u, d)
        for d in (
            jnp.minimum(d_e, d_ee),
            d_w,
            jnp.minimum(d_n, d_ne),
            jnp.minimum(d_s, d_se),
        )
    ]
    v_neighbours = [
        jnp.minimum(d_v, d)
        for d in (
            jnp.minimum(d_e, d_ne),
            jnp.minimum(d_w, d_nw),
            jnp.minimum(d_n, d_nn),
            d_s,
        )
    ]

    level_row = lax.broadcasted_iota(jnp.int32, (levels, lanes), 0)
    level_lane = lax.broadcasted_iota(jnp.int32, (levels, lanes), 1)
    wet_row = jnp.minimum(
        west_ref[pl.ds(depth_at, 1), :], depth_ref[pl.ds(0, 1), :]
    )
    wet_face = level_row.astype(jnp.float32) < wet_row
    u_west = west_ref[pl.ds(4 * levels, levels), :]
    for place, field, target in ((0, t_ref, gx_t_ref), (2, s_ref, gx_s_ref)):
        near = west_ref[pl.ds(place * levels, levels), :]
        far = west_ref[pl.ds((place + 1) * levels, levels), :]
        own = field[:, 0, :]
        face = u_west * (1.0 / 12.0) * (7.0 * (near + own) - (far + field[:, 1, :]))
        target[...] = jnp.where(wet_face, face - TRACER_DIFF * (own - near), 0.0)

    def column(corner, place):
        picked = jnp.where(level_lane == 3 * (place * levels + level_row) + 2, corner[0:1], 0.0)
        return jnp.sum(picked, axis=1, keepdims=True)

    u_corner = column(nw_uv, 0)
    v_corner = column(se_uv, 1)
    u2_ref[...] = u_west + jnp.where(
        level_lane == lanes - 1, u_corner, pltpu.roll(u_west, lanes - 1, 1)
    )
    v_east = east_ref[pl.ds(5 * levels, levels), :]
    v2_ref[...] = v_east + jnp.where(level_lane == 0, v_corner, pltpu.roll(v_east, 1, 1))

    in_block = jnp.where(lane < 3 * levels, lane, lane - 3 * levels).astype(jnp.float32)
    v_south = jnp.where(lane < 3 * levels, at_south(south_uv, 3 * levels), south_uv)
    both = south + bottom
    face = v_south * (1.0 / 12.0) * (7.0 * both - pltpu.roll(both, 1, 1))
    face = face - TRACER_DIFF * (bottom - south)
    wet_south = jnp.minimum(
        south[:, count_at : count_at + 1], bottom[:, count_at : count_at + 1]
    )
    face_south = jnp.where(in_block < 3.0 * wet_south, face, 0.0)

    third = lax.rem(lane, 3)
    near, near_uv = (
        jnp.where(third == 0, pltpu.roll(s, 1, 1), n)
        for n, s in ((north, south), (north_uv, south_uv))
    )
    far = jnp.where(third == 2, face_south, north)
    for place in range(2):
        for k in range(levels):
            spot = 3 * (place * levels + k) + 2
            near_ref[place * levels + k] = at_north(near, spot)
            near_ref[(place + 2) * levels + k] = at_north(near_uv, spot)
            far_ref[place * levels + k] = at_north(far, spot - 1)

    row_id = (lat * lanes + lane).astype(jnp.float32)
    total = float(lat_count * lanes)
    cor_u = 2.0 * (row_id + 0.5) / total - 1.0
    cor_v = 2.0 * (row_id + 1.0) / total - 1.0
    inner, last = mixing_constants(levels)
    gain = TIME_STEP * VERTICAL_VISC

    def masked(k, count, value):
        return jnp.where(float(k) < count, value, 0.0)

    px = jnp.zeros((SUB, lanes), jnp.float32)
    py = jnp.zeros((SUB, lanes), jnp.float32)
    above = None
    ratio = None
    values = None
    for k in range(levels):
        u = tall(u_ref[k])
        v = tall(v_ref[k])
        u_face = masked(k, d_u, u * (1.0 / 12.0))
        u_diff = masked(k, d_u, TRACER_DIFF)
        v_face = masked(k, d_v, v * (1.0 / 12.0))
        v_diff = masked(k, d_v, TRACER_DIFF)
        stars = []
        seen = []
        for place, field, gx_ref in ((0, t_ref, gx_t_ref), (2, s_ref, gx_s_ref)):
            near, far = place * levels + k, (place + 1) * levels + k
            c = tall(field[k])
            c_e = to_east(c, line(east_ref, near))
            c_ee = to_east(c_e, line(east_ref, far))
            c_w = to_west(c, line(west_ref, near))
            beyond = near_ref[place // 2 * levels + k]
            c_n = to_north(c, beyond)
            beyond_2 = far_ref[place // 2 * levels + k]
            c_nn = to_north(c_n, beyond_2)
            c_s = to_south(c, beyond)
            gx = u_face * (7.0 * (c + c_e) - (c_w + c_ee)) - u_diff * (c_e - c)
            gy = v_face * (7.0 * (c + c_n) - (c_s + c_nn)) - v_diff * (c_n - c)
            gx_w = to_west(gx, line(gx_ref, k))
            gy_s = to_south(gy, beyond_2)
            stars.append(c - TIME_STEP * masked(k, depth, (gx - gx_w) + (gy - gy_s)))
            seen.append((c, c_e, c_n))
        weights = THERMAL_EXPANSION, HALINE_CONTRACTION
        b, b_e, b_n = (
            masked(k, d, weights[0] * warm - weights[1] * salt)
            for d, warm, salt in zip((depth, d_e, d_n), seen[0], seen[1])
        )
        bx = b_e - b
        by = b_n - b
        px = px + bx
        py = py + by

        u_e = to_east(u, line(east_ref, 4 * levels + k))
        u_w = to_west(u, line(west_ref, 4 * levels + k))
        u_n = to_north(u, near_ref[2 * levels + k])
        u_s = to_south(u, near_ref[2 * levels + k])
        v_e = to_east(v, line(east_ref, 5 * levels + k))
        v_w = to_west(v, line(west_ref, 5 * levels + k))
        v_n = to_north(v, near_ref[3 * levels + k])
        v_s = to_south(v, near_ref[3 * levels + k])
        v2 = v + v_s
        u2 = u + u_n
        v_bar = 0.25 * (v2 + to_east(v2, line(v2_ref, k)))
        u_bar = 0.25 * (u2 + to_west(u2, line(u2_ref, k)))
        u_visc = sum(masked(k, d, n - u) for d, n in zip(u_neighbours, (u_e, u_w, u_n, u_s)))
        v_visc = sum(masked(k, d, n - v) for d, n in zip(v_neighbours, (v_e, v_w, v_n, v_s)))
        u_star = u + TIME_STEP * (cor_u * v_bar - (px - 0.5 * bx) + MOMENTUM_VISC * u_visc)
        v_star = v + TIME_STEP * (-cor_v * u_bar - (py - 0.5 * by) + MOMENTUM_VISC * v_visc)
        if k == 0:
            u_star = u_star + TIME_STEP * WIND_GAIN * tall(wind_ref[0])
            v_star = v_star + TIME_STEP * WIND_GAIN * tall(wind_ref[1])

        if k < levels - 1:
            below = masked(k + 1, depth, TIME_STEP * tall(mix_ref[k]))
        else:
            below = None
        pivot = 1.0
        if above is not None:
            pivot = pivot + above * (1.0 - ratio)
        if below is not None:
            pivot = pivot + below
        inverse = 1.0 / pivot

        def momentum_weight(count):
            weight = jnp.where(float(k) < count, last[k], 0.0)
            if k < levels - 1:
                weight = jnp.where(float(k + 1) < count, inner[k], weight)
            return weight

        rights = stars + [u_star, v_star]
        scales = [inverse, inverse, momentum_weight(d_u), momentum_weight(d_v)]
        if k > 0:
            gains = [above, above, gain, gain]
            rights = [right + g * value for right, g, value in zip(rights, gains, values)]
        values = [right * scale for right, scale in zip(rights, scales)]
        for index, value in enumerate(values):
            val_ref[index, k] = value
        if below is not None:
            ratio = below * inverse
            val_ref[4, k] = ratio
        above = below

    outs = (t_out, s_out, u_out, v_out)
    for k in range(levels - 1, -1, -1):
        if k < levels - 1:
            ratios = [val_ref[4, k], val_ref[4, k], gain * inner[k], gain * inner[k]]
            values = [val_ref[i, k] + ratios[i] * values[i] for i in range(4)]
        for out, value in zip(outs, values):
            out[k] = value[:width]


def shards(
    thermal_anomaly,
    saltiness_anomaly,
    zonal_current,
    meridional_current,
    bottom_ocean_layer,
    seam_axis_meridian,
    interface_diffusivity,
    atmospheric_forcing,
):
    levels, width, lanes = thermal_anomaly.shape
    lon_count = lax.axis_size("lon")
    lat_count = lax.axis_size("lat")
    fields = (thermal_anomaly, saltiness_anomaly, zonal_current, meridional_current)
    wind = atmospheric_forcing
    f32 = jnp.float32
    row_message = jax.ShapeDtypeStruct((2 * width, lanes), f32)
    column_message = jax.ShapeDtypeStruct((6 * levels + 8, lanes), f32)

    fold_message = jax.ShapeDtypeStruct((6 * levels + 16, lanes), f32)
    lat_pairs = [
        [(a, b) for i in range(start, lat_count - 1, 2) for a, b in ((i, i + 1), (i + 1, i))]
        for start in (0, 1)
    ]
    lat_pairs = [pairs for pairs in lat_pairs if pairs]
    top, bottom, eastward, westward, counts, stress, *messages = pl.pallas_call(
        edges_kernel,
        out_shape=[row_message] * 2
        + [column_message] * 2
        + [jax.ShapeDtypeStruct((width, lanes), f32), jax.ShapeDtypeStruct(wind.shape, f32)]
        + [jax.ShapeDtypeStruct((4 * width, lanes), f32), row_message][: len(lat_pairs)],
        in_specs=[VMEM] * 6,
        out_specs=[VMEM] * (6 + len(lat_pairs)),
        compiler_params=FIRST,
    )(*[pltpu.with_memory_space_constraint(x, pltpu.HBM) for x in (*fields, bottom_ocean_layer, wind)])
    received = [
        lax.ppermute(message, "lat", pairs) for message, pairs in zip(messages, lat_pairs)
    ]

    north, south, eastward, fold, westward, rest = pl.pallas_call(
        corners_kernel,
        out_shape=[row_message] * 2
        + [column_message, fold_message, column_message]
        + [jax.ShapeDtypeStruct((SUB, lanes), jnp.int32)],
        in_specs=[VMEM] * 3 + [SMEM] + [VMEM] * len(received),
        out_specs=[VMEM] * 6,
        compiler_params=SMALL,
    )(top, eastward, westward, seam_axis_meridian, *received)

    code = seam_axis_meridian[0]
    tile = lax.rem(lax.div(code, width), lon_count)
    three = (lax.rem(code, width) == width - 1).astype(jnp.int32)
    ring = [(i, (i + 1) % lon_count) for i in range(lon_count)]
    trade = [(i, i ^ 1) for i in range(lon_count)]
    pairs = [(i, i ^ 1) for i in range(lat_count)]

    def fold_pairs(*mirrors):
        rows = [*mirrors] + [trade] * (lat_count - len(mirrors))
        return [
            (a * lat_count + lat_count - 1 - row, b * lat_count + lat_count - 1 - row)
            for row, mirror in enumerate(rows)
            for a, b in mirror
        ]

    from_west = lax.ppermute(eastward, "lon", ring)
    keep = pl.pallas_call(
        keep_kernel,
        out_shape=column_message,
        in_specs=[VMEM],
        out_specs=VMEM,
        compiler_params=SMALL,
    )

    def reflect(code):
        own = [i for i in range(lon_count) if (code - i) % lon_count == i]
        if len(own) != 2:
            return [(i, (code - i) % lon_count) for i in range(lon_count)], []
        trade = {own[0]: own[1], own[1]: own[0]}
        return [(i, trade.get(i, (code - i) % lon_count)) for i in range(lon_count)], own

    def exchange(first, count):
        direct = first % 2
        mirrors, own_tiles = zip(*(reflect(first - 1 + d) for d in range(3)))
        mirror = pl.pallas_call(
            functools.partial(mirror_kernel, own_tiles),
            out_shape=jax.ShapeDtypeStruct((2, 16, lanes), f32),
            in_specs=[VMEM] * (2 + count),
            out_specs=VMEM,
            scratch_shapes=[pltpu.VMEM((2, 3 * width, lanes), f32)],
            compiler_params=SMALL,
        )

        def branch(fold, westward, rest):
            both = ("lon", "lat")
            tile = lax.ppermute(fold, both, fold_pairs(mirrors[direct], mirrors[1 - direct]))
            tiles = [tile, lax.ppermute(tile[: 2 * width], "lat", pairs)]
            if direct == 1:
                tiles = tiles[::-1]
            if count == 3:
                tiles.append(lax.ppermute(fold, both, fold_pairs(mirrors[2])))
            return (
                keep(lax.ppermute(westward, "lon", [(b, a) for a, b in ring])),
                mirror(fold, rest, *tiles),
            )

        return branch

    branches = [exchange(first, count) for first in range(lon_count) for count in (2, 3)]
    from_east, mirrored = lax.switch(
        tile * 2 + three, branches, fold, westward, rest
    )

    whole = jax.ShapeDtypeStruct((levels, width, lanes), f32)
    return pl.pallas_call(
        step_kernel,
        out_shape=[whole] * 4,
        in_specs=[VMEM] * 13,
        out_specs=[VMEM] * 4,
        compiler_params=LARGE,
        scratch_shapes=[pltpu.VMEM((levels, lanes), f32)] * 4
        + [pltpu.VMEM((5, levels, SUB, lanes), f32)]
        + [pltpu.VMEM((count * levels, SUB, lanes), f32) for count in (4, 2)],
    )(
        *fields,
        counts,
        interface_diffusivity,
        stress,
        bottom,
        north,
        south,
        from_west,
        from_east,
        mirrored,
    )


def solution(mesh):
    split = P(None, "lon", "lat")
    return jax.shard_map(
        shards,
        mesh=mesh,
        in_specs=(split, split, split, split, P("lon", "lat"), P(), split, split),
        out_specs=(split, split, split, split),
        check_vma=False,
    )
```

profile of v0, /device:TPU:0, one launch (start us, length us, event | category | flops | bytes accessed | tf_op | source)
XLA Modules:
  0.0 15.4 jit_solution(9483369325426754331)
XLA Ops:
  0.6 1.2 %shard_map.111 = (f32[16,128]{1,0:T(8,128)S(1)}, f32[16,128]{1,0:T(8,128)S(1)}, f32[104,128]{1,0:T(8,128)S(1)}, f32[104,128]{1,0:T(8,128)S(1)}, f32[8,128]{1,0:T...) custom-call(f32[16,8,128]{2,1,0:T(8,128)} %t_ref.3, f32[16,8,128]{2,1,0:T(8,128)} %s_ref.3, ...), custom_call_target="tpu_custom_call" | custom-call | tf_op jit(solution)/shard_map/pallas_call | solution.py:469
  1.8 0.5 %collective-permute-start.112 = (f32[32,128]{1,0:T(8,128)S(1)}, f32[32,128]{1,0:T(8,128)S(1)}, u32[]{:S(2)}, u32[]{:S(2)}) collective-permute-start(f32[32,128]{1,0:T(8,128)S(1)} %get-tuple-element.313), channel_id=1, source_target_pairs={{0,1},{1,0},{2,3},{3,2},{4,5},{5,4},{6,7},{7,6},{8,9},{9,8},{10,11... | collective-permute-start | bytes 49160 | tf_op jit(solution)/shard_map/ppermute | solution.py:480
  3.0 0.2 %collective-permute-done.112.refs_0_ = f32[32,128]{1,0:T(8,128)S(1)} collective-permute-done((f32[32,128]{1,0:T(8,128)S(1)}, f32[32,128]{1,0:T(8,128)S(1)}, u32[]{:S(2)}, u32[]{:S(2)}) %collective-permute-start.112) | collective-permute-done | bytes 16416 | tf_op jit(solution)/shard_map/ppermute | solution.py:480
  3.2 0.1 shard_map.112
  3.2 2.8 %collective-permute-start.113 = (f32[104,128]{1,0:T(8,128)S(1)}, f32[104,128]{1,0:T(8,128)S(1)}, u32[]{:S(2)}, u32[]{:S(2)}) collective-permute-start(f32[104,128]{1,0:T(8,128)S(1)} %get-tuple-element.316), channel_id=1, source_target_pairs={{0,2},{2,4},{4,6},{6,8},{8,10},{10,12},{12,14},{14,16},{16,18},{18... | collective-permute-start | bytes 159752 | tf_op jit(solution)/shard_map/ppermute | solution.py:508
  6.1 0.0 copy-start
  6.1 0.0 copy-start.1
  6.1 0.0 copy-start.2
  6.1 0.0 copy-start.3
  6.1 0.0 copy-start.4
  6.1 7.7 %conditional.1 = (f32[104,128]{1,0:T(8,128)S(1)}, f32[2,16,128]{2,1,0:T(8,128)S(1)}) conditional(s32[]{:T(128)} %clamp.3, (f32[104,128]{1,0:T(8,128)S(1)}, f32[112,128]{1,0:T(8,128)S(1)}, s32[8,128]{1,0:T(8,128)S(1)}) %tuple.135, (f32[104,128]{1,0:T(8,128)S(1)}, f32[112,128]{1,0:T(8,128)S(1)}, ...), branch_computations={%region_0.0_spmd, %region_1.0_spmd, %region_2.0_spmd, %region_3.0_... | conditional | bytes 721072 | solution.py:552
  6.1 1.6 %collective-permute-start.22 = (f32[112,128]{1,0:T(8,128)S(1)}, f32[112,128]{1,0:T(8,128)S(1)}, u32[]{:S(2)}, u32[]{:S(2)}) collective-permute-start(f32[112,128]{1,0:T(8,128)S(1)} %get-tuple-element.211.own_ref), channel_id=1, source_target_pairs={{1,7},{3,5},{5,3},{7,1},{9,31},{11,29},{13,27},{15,25},{17,23},{19... | collective-permute-start | bytes 172040 | tf_op jit(solution)/shard_map/cond/branch_6_fun/ppermute | solution.py:538
  7.7 4.2 %collective-permute-start.21 = (f32[104,128]{1,0:T(8,128)S(1)}, f32[104,128]{1,0:T(8,128)S(1)}, u32[]{:S(2)}, u32[]{:S(2)}) collective-permute-start(f32[104,128]{1,0:T(8,128)S(1)} %get-tuple-element.210), channel_id=1, source_target_pairs={{2,0},{4,2},{6,4},{8,6},{10,8},{12,10},{14,12},{16,14},{18,16},{20... | collective-permute-start | bytes 159752 | tf_op jit(solution)/shard_map/cond/branch_6_fun/ppermute | solution.py:545
  11.9 0.0 collective-permute-done.22.refs_1_
  11.9 0.0 collective-permute-start.23
  11.9 1.8 %collective-permute-done.21.message_ref = f32[104,128]{1,0:T(8,128)S(1)} collective-permute-done((f32[104,128]{1,0:T(8,128)S(1)}, f32[104,128]{1,0:T(8,128)S(1)}, u32[]{:S(2)}, u32[]{:S(2)}) %collective-permute-start.21) | collective-permute-done | bytes 53280 | tf_op jit(solution)/shard_map/cond/branch_6_fun/ppermute | solution.py:545
  13.7 0.0 collective-permute-done.23.refs_0_
  13.8 0.0 collective-permute-done.113.west_ref
  13.8 0.0 copy-done
  13.8 0.0 copy-done.1
  13.8 0.0 copy-done.2
  13.8 0.0 copy-done.3
  13.8 0.0 copy-done.4
  13.8 1.5 %shard_map.113 = (f32[16,8,128]{2,1,0:T(8,128)}, f32[16,8,128]{2,1,0:T(8,128)}, f32[16,8,128]{2,1,0:T(8,128)}, f32[16,8,128]{2,1,0:T(8,128)}) custom-call(f32[16,8,128]{2,1,0:T(8,128)S(1)} %copy-done, f32[16,8,128]{2,1,0:T(8,128)S(1)} %copy-done.1, f32[16,8,128]{2,1,0:T(8,128)S(1)} %copy-done.2, f32[16,8,128]{2,1,0:T(8,128)S(1)} %copy-done.3, ...), custom_call_target="tpu_custom_call" | custom-call | tf_op jit(solution)/shard_map/pallas_call | solution.py:557
  (3 shorter events, 0.1 us)
Async XLA Ops:
  1.8 1.3 %collective-permute-start.112 = (f32[32,128]{1,0:T(8,128)S(1)}, f32[32,128]{1,0:T(8,128)S(1)}, u32[]{:S(2)}, u32[]{:S(2)}) collective-permute-start(f32[32,128]{1,0:T(8,128)S(1)} %get-tuple-element.313), channel_id=1, source_target_pairs={{0,1},{1,0},{2,3},{3,2},{4,5},{5,4},{6,7},{7,6},{8,9},{9,8},{10,11... | collective-permute-start | bytes 49160 | tf_op jit(solution)/shard_map/ppermute | solution.py:480
  3.2 10.5 %collective-permute-start.113 = (f32[104,128]{1,0:T(8,128)S(1)}, f32[104,128]{1,0:T(8,128)S(1)}, u32[]{:S(2)}, u32[]{:S(2)}) collective-permute-start(f32[104,128]{1,0:T(8,128)S(1)} %get-tuple-element.316), channel_id=1, source_target_pairs={{0,2},{2,4},{4,6},{6,8},{8,10},{10,12},{12,14},{14,16},{16,18},{18... | collective-permute-start | bytes 159752 | tf_op jit(solution)/shard_map/ppermute | solution.py:508
  6.1 7.7 %copy-start = (f32[16,8,128]{2,1,0:T(8,128)S(1)}, f32[16,8,128]{2,1,0:T(8,128)}, u32[]{:S(2)}) copy-start(f32[16,8,128]{2,1,0:T(8,128)} %t_ref.3) | copy-start | bytes 196612
  6.1 7.7 %copy-start.1 = (f32[16,8,128]{2,1,0:T(8,128)S(1)}, f32[16,8,128]{2,1,0:T(8,128)}, u32[]{:S(2)}) copy-start(f32[16,8,128]{2,1,0:T(8,128)} %s_ref.3) | copy-start | bytes 196612
  6.1 7.7 %copy-start.2 = (f32[16,8,128]{2,1,0:T(8,128)S(1)}, f32[16,8,128]{2,1,0:T(8,128)}, u32[]{:S(2)}) copy-start(f32[16,8,128]{2,1,0:T(8,128)} %u_ref.3) | copy-start | bytes 196612
  6.1 7.8 %copy-start.3 = (f32[16,8,128]{2,1,0:T(8,128)S(1)}, f32[16,8,128]{2,1,0:T(8,128)}, u32[]{:S(2)}) copy-start(f32[16,8,128]{2,1,0:T(8,128)} %v_ref.3) | copy-start | bytes 196612
  6.1 7.8 %copy-start.4 = (f32[15,8,128]{2,1,0:T(8,128)S(1)}, f32[15,8,128]{2,1,0:T(8,128)}, u32[]{:S(2)}) copy-start(f32[15,8,128]{2,1,0:T(8,128)} %mix_ref.1) | copy-start | bytes 184324
  6.1 5.8 %collective-permute-start.22 = (f32[112,128]{1,0:T(8,128)S(1)}, f32[112,128]{1,0:T(8,128)S(1)}, u32[]{:S(2)}, u32[]{:S(2)}) collective-permute-start(f32[112,128]{1,0:T(8,128)S(1)} %get-tuple-element.211.own_ref), channel_id=1, source_target_pairs={{1,7},{3,5},{5,3},{7,1},{9,31},{11,29},{13,27},{15,25},{17,23},{19... | collective-permute-start | bytes 172040 | tf_op jit(solution)/shard_map/cond/branch_6_fun/ppermute | solution.py:538
  7.7 6.0 %collective-permute-start.21 = (f32[104,128]{1,0:T(8,128)S(1)}, f32[104,128]{1,0:T(8,128)S(1)}, u32[]{:S(2)}, u32[]{:S(2)}) collective-permute-start(f32[104,128]{1,0:T(8,128)S(1)} %get-tuple-element.210), channel_id=1, source_target_pairs={{2,0},{4,2},{6,4},{8,6},{10,8},{12,10},{14,12},{16,14},{18,16},{20... | collective-permute-start | bytes 159752 | tf_op jit(solution)/shard_map/cond/branch_6_fun/ppermute | solution.py:545
  11.9 1.8 %collective-permute-start.23 = (f32[16,128]{1,0:T(8,128)S(1)}, f32[16,128]{1,0:T(8,128)S(1)}, u32[]{:S(2)}, u32[]{:S(2)}) collective-permute-start(f32[16,128]{1,0:T(8,128)S(1)} %slice.102), channel_id=1, source_target_pairs={{0,1},{1,0},{2,3},{3,2},{4,5},{5,4},{6,7},{7,6},{8,9},{9,8},{10,11... | collective-permute-start | bytes 24584 | tf_op jit(solution)/shard_map/cond/branch_6_fun/ppermute | solution.py:539
where the time goes:
time: 15.7 us; the launch traced here: 15.4 us
  starting transfers between devices  9.11 us (58%)
  Pallas kernels  2.85 us (18%)
  waiting for transfers between devices  1.97 us (13%)
  between operations  1.35 us (9%)
    ppermute x1, starting transfers between devices, branch(): lax.ppermute(westward, 'lon', [(b, a) for a, b in ring])  4.19 us
    ppermute x1, starting transfers between devices, shards(): from_west = lax.ppermute(eastward, 'lon', ring)  2.83 us
    ppermute x1, waiting for transfers between devices, branch(): lax.ppermute(westward, 'lon', [(b, a) for a, b in ring])  1.78 us
    ppermute x1, starting transfers between devices, branch(): lax.ppermute(fold, both, fold_pairs(mirrors[direct], mirrors[1 - direct]))  1.58 us
    pallas_call x1, Pallas kernels, shards(): pl.pallas_call(step_kernel, out_shape=[whole] * 4, in_specs=[VMEM] * 13,...  1.53 us
    pallas_call x1, Pallas kernels, shards(): pl.pallas_call(edges_kernel, out_shape=[row_message] * 2 + [column_messag...  1.18 us
    ppermute x1, starting transfers between devices, shards(): lax.ppermute(message, 'lat', pairs)  0.5 us
  transfers between devices with their start and end apart: 5, of which 2 were waited for; matrix products, arithmetic and copies ran while one was open for 0% of the time, Pallas kernels for 0%

commit v1 on v0

--- a/solution.py
+++ b/solution.py
@@ -64,8 +64,8 @@
     for first, second, count in ((t_ref, s_ref, depth_ref), (u_ref, v_ref, None)):
         top = jnp.zeros((SUB, lanes), jnp.float32)
         bottom = jnp.zeros((SUB, lanes), jnp.float32)
-        places = [(3 * k, first, k) for k in range(levels)]
-        places += [(3 * (levels + k), second, k) for k in range(levels)]
+        places = [(3 * (levels - 1 - k), first, k) for k in range(levels)]
+        places += [(3 * (2 * levels - 1 - k), second, k) for k in range(levels)]
         if count is not None:
             places.append((6 * levels, count, None))
         for start, ref, k in places:
@@ -296,12 +296,13 @@
         face = u_west * (1.0 / 12.0) * (7.0 * (near + own) - (far + field[:, 1, :]))
         target[...] = jnp.where(wet_face, face - TRACER_DIFF * (own - near), 0.0)
 
-    def column(corner, place):
-        picked = jnp.where(level_lane == 3 * (place * levels + level_row) + 2, corner[0:1], 0.0)
-        return jnp.sum(picked, axis=1, keepdims=True)
-
-    u_corner = column(nw_uv, 0)
-    v_corner = column(se_uv, 1)
+    def spread(corner, place, target):
+        lines = jnp.broadcast_to(corner[0:1], (levels, lanes))
+        shift = target - (3 * ((place + 1) * levels - 1) + 2)
+        return pltpu.roll(lines, shift % lanes, 1, stride=3, stride_axis=0)
+
+    u_corner = spread(nw_uv, 0, lanes - 1)
+    v_corner = spread(se_uv, 1, 0)
     u2_ref[...] = u_west + jnp.where(
         level_lane == lanes - 1, u_corner, pltpu.roll(u_west, lanes - 1, 1)
     )
@@ -316,7 +317,7 @@
     wet_south = jnp.minimum(
         south[:, count_at : count_at + 1], bottom[:, count_at : count_at + 1]
     )
-    face_south = jnp.where(in_block < 3.0 * wet_south, face, 0.0)
+    face_south = jnp.where(in_block > 3.0 * (levels - wet_south), face, 0.0)
 
     third = lax.rem(lane, 3)
     near, near_uv = (
@@ -326,7 +327,7 @@
     far = jnp.where(third == 2, face_south, north)
     for place in range(2):
         for k in range(levels):
-            spot = 3 * (place * levels + k) + 2
+            spot = 3 * ((place + 1) * levels - 1 - k) + 2
             near_ref[place * levels + k] = at_north(near, spot)
             near_ref[(place + 2) * levels + k] = at_north(near_uv, spot)
             far_ref[place * levels + k] = at_north(far, spot - 1)

time: 15.7 us -> 15.5 us (0.987); the launches traced: 15.4 us -> 15.3 us
  no operation moved by 1% of the time
where the time goes in v1:
time: 15.5 us; the launch traced here: 15.3 us
  starting transfers between devices  9.16 us (59%)
  Pallas kernels  2.76 us (18%)
  waiting for transfers between devices  1.97 us (13%)
  between operations  1.35 us (9%)
    ppermute x1, starting transfers between devices, branch(): lax.ppermute(westward, 'lon', [(b, a) for a, b in ring])  4.19 us
    ppermute x1, starting transfers between devices, shards(): from_west = lax.ppermute(eastward, 'lon', ring)  2.83 us
    ppermute x1, waiting for transfers between devices, branch(): lax.ppermute(westward, 'lon', [(b, a) for a, b in ring])  1.78 us
    ppermute x1, starting transfers between devices, branch(): lax.ppermute(fold, both, fold_pairs(mirrors[direct], mirrors[1 - direct]))  1.64 us
    pallas_call x1, Pallas kernels, shards(): pl.pallas_call(step_kernel, out_shape=[whole] * 4, in_specs=[VMEM] * 13,...  1.43 us
    pallas_call x1, Pallas kernels, shards(): pl.pallas_call(edges_kernel, out_shape=[row_message] * 2 + [column_messag...  1.19 us
    ppermute x1, starting transfers between devices, shards(): lax.ppermute(message, 'lat', pairs)  0.5 us
  transfers between devices with their start and end apart: 5, of which 2 were waited for; matrix products, arithmetic and copies ran while one was open for 0% of the time, Pallas kernels for 0%

profile of v1, /device:TPU:0, one launch (start us, length us, event | category | flops | bytes accessed | tf_op | source)
XLA Modules:
  0.0 15.3 jit_solution(12236773668377881908)
XLA Ops:
  0.6 1.2 %shard_map.111 = (f32[16,128]{1,0:T(8,128)S(1)}, f32[16,128]{1,0:T(8,128)S(1)}, f32[104,128]{1,0:T(8,128)S(1)}, f32[104,128]{1,0:T(8,128)S(1)}, f32[8,128]{1,0:T...) custom-call(f32[16,8,128]{2,1,0:T(8,128)} %t_ref.3, f32[16,8,128]{2,1,0:T(8,128)} %s_ref.3, ...), custom_call_target="tpu_custom_call" | custom-call | tf_op jit(solution)/shard_map/pallas_call | solution.py:470
  1.8 0.5 %collective-permute-start.112 = (f32[32,128]{1,0:T(8,128)S(1)}, f32[32,128]{1,0:T(8,128)S(1)}, u32[]{:S(2)}, u32[]{:S(2)}) collective-permute-start(f32[32,128]{1,0:T(8,128)S(1)} %get-tuple-element.313), channel_id=1, source_target_pairs={{0,1},{1,0},{2,3},{3,2},{4,5},{5,4},{6,7},{7,6},{8,9},{9,8},{10,11... | collective-permute-start | bytes 49160 | tf_op jit(solution)/shard_map/ppermute | solution.py:481
  3.0 0.2 %collective-permute-done.112.refs_0_ = f32[32,128]{1,0:T(8,128)S(1)} collective-permute-done((f32[32,128]{1,0:T(8,128)S(1)}, f32[32,128]{1,0:T(8,128)S(1)}, u32[]{:S(2)}, u32[]{:S(2)}) %collective-permute-start.112) | collective-permute-done | bytes 16416 | tf_op jit(solution)/shard_map/ppermute | solution.py:481
  3.2 0.1 shard_map.112
  3.2 2.8 %collective-permute-start.113 = (f32[104,128]{1,0:T(8,128)S(1)}, f32[104,128]{1,0:T(8,128)S(1)}, u32[]{:S(2)}, u32[]{:S(2)}) collective-permute-start(f32[104,128]{1,0:T(8,128)S(1)} %get-tuple-element.316), channel_id=1, source_target_pairs={{0,2},{2,4},{4,6},{6,8},{8,10},{10,12},{12,14},{14,16},{16,18},{18... | collective-permute-start | bytes 159752 | tf_op jit(solution)/shard_map/ppermute | solution.py:509
  6.1 0.0 copy-start
  6.1 0.0 copy-start.1
  6.1 0.0 copy-start.2
  6.1 0.0 copy-start.3
  6.1 0.0 copy-start.4
  6.1 7.7 %conditional.1 = (f32[104,128]{1,0:T(8,128)S(1)}, f32[2,16,128]{2,1,0:T(8,128)S(1)}) conditional(s32[]{:T(128)} %clamp.3, (f32[104,128]{1,0:T(8,128)S(1)}, f32[112,128]{1,0:T(8,128)S(1)}, s32[8,128]{1,0:T(8,128)S(1)}) %tuple.135, (f32[104,128]{1,0:T(8,128)S(1)}, f32[112,128]{1,0:T(8,128)S(1)}, ...), branch_computations={%region_0.0_spmd, %region_1.0_spmd, %region_2.0_spmd, %region_3.0_... | conditional | bytes 721072 | solution.py:553
  6.1 1.6 %collective-permute-start.36 = (f32[112,128]{1,0:T(8,128)S(1)}, f32[112,128]{1,0:T(8,128)S(1)}, u32[]{:S(2)}, u32[]{:S(2)}) collective-permute-start(f32[112,128]{1,0:T(8,128)S(1)} %get-tuple-element.223.own_ref), channel_id=1, source_target_pairs={{1,11},{3,9},{5,7},{7,5},{9,3},{11,1},{13,31},{15,29},{17,27},{19,... | collective-permute-start | bytes 172040 | tf_op jit(solution)/shard_map/cond/branch_10_fun/ppermute | solution.py:539
  7.8 4.2 %collective-permute-start.35 = (f32[104,128]{1,0:T(8,128)S(1)}, f32[104,128]{1,0:T(8,128)S(1)}, u32[]{:S(2)}, u32[]{:S(2)}) collective-permute-start(f32[104,128]{1,0:T(8,128)S(1)} %get-tuple-element.222), channel_id=1, source_target_pairs={{2,0},{4,2},{6,4},{8,6},{10,8},{12,10},{14,12},{16,14},{18,16},{20... | collective-permute-start | bytes 159752 | tf_op jit(solution)/shard_map/cond/branch_10_fun/ppermute | solution.py:546
  12.0 0.0 collective-permute-done.36.refs_1_
  12.0 0.0 collective-permute-start.37
  12.0 1.8 %collective-permute-done.35.message_ref = f32[104,128]{1,0:T(8,128)S(1)} collective-permute-done((f32[104,128]{1,0:T(8,128)S(1)}, f32[104,128]{1,0:T(8,128)S(1)}, u32[]{:S(2)}, u32[]{:S(2)}) %collective-permute-start.35) | collective-permute-done | bytes 53280 | tf_op jit(solution)/shard_map/cond/branch_10_fun/ppermute | solution.py:546
  13.8 0.0 collective-permute-done.37.refs_0_
  13.8 0.0 collective-permute-done.113.west_ref
  13.9 0.0 copy-done
  13.9 0.0 copy-done.1
  13.9 0.0 copy-done.2
  13.9 0.0 copy-done.3
  13.9 0.0 copy-done.4
  13.9 1.4 %shard_map.113 = (f32[16,8,128]{2,1,0:T(8,128)}, f32[16,8,128]{2,1,0:T(8,128)}, f32[16,8,128]{2,1,0:T(8,128)}, f32[16,8,128]{2,1,0:T(8,128)}) custom-call(f32[16,8,128]{2,1,0:T(8,128)S(1)} %copy-done, f32[16,8,128]{2,1,0:T(8,128)S(1)} %copy-done.1, f32[16,8,128]{2,1,0:T(8,128)S(1)} %copy-done.2, f32[16,8,128]{2,1,0:T(8,128)S(1)} %copy-done.3, ...), custom_call_target="tpu_custom_call" | custom-call | tf_op jit(solution)/shard_map/pallas_call | solution.py:558
  (3 shorter events, 0.1 us)
Async XLA Ops:
  1.8 1.3 %collective-permute-start.112 = (f32[32,128]{1,0:T(8,128)S(1)}, f32[32,128]{1,0:T(8,128)S(1)}, u32[]{:S(2)}, u32[]{:S(2)}) collective-permute-start(f32[32,128]{1,0:T(8,128)S(1)} %get-tuple-element.313), channel_id=1, source_target_pairs={{0,1},{1,0},{2,3},{3,2},{4,5},{5,4},{6,7},{7,6},{8,9},{9,8},{10,11... | collective-permute-start | bytes 49160 | tf_op jit(solution)/shard_map/ppermute | solution.py:481
  3.2 10.6 %collective-permute-start.113 = (f32[104,128]{1,0:T(8,128)S(1)}, f32[104,128]{1,0:T(8,128)S(1)}, u32[]{:S(2)}, u32[]{:S(2)}) collective-permute-start(f32[104,128]{1,0:T(8,128)S(1)} %get-tuple-element.316), channel_id=1, source_target_pairs={{0,2},{2,4},{4,6},{6,8},{8,10},{10,12},{12,14},{14,16},{16,18},{18... | collective-permute-start | bytes 159752 | tf_op jit(solution)/shard_map/ppermute | solution.py:509
  6.1 7.8 %copy-start = (f32[16,8,128]{2,1,0:T(8,128)S(1)}, f32[16,8,128]{2,1,0:T(8,128)}, u32[]{:S(2)}) copy-start(f32[16,8,128]{2,1,0:T(8,128)} %t_ref.3) | copy-start | bytes 196612
  6.1 7.8 %copy-start.1 = (f32[16,8,128]{2,1,0:T(8,128)S(1)}, f32[16,8,128]{2,1,0:T(8,128)}, u32[]{:S(2)}) copy-start(f32[16,8,128]{2,1,0:T(8,128)} %s_ref.3) | copy-start | bytes 196612
  6.1 7.8 %copy-start.2 = (f32[16,8,128]{2,1,0:T(8,128)S(1)}, f32[16,8,128]{2,1,0:T(8,128)}, u32[]{:S(2)}) copy-start(f32[16,8,128]{2,1,0:T(8,128)} %u_ref.3) | copy-start | bytes 196612
  6.1 7.8 %copy-start.3 = (f32[16,8,128]{2,1,0:T(8,128)S(1)}, f32[16,8,128]{2,1,0:T(8,128)}, u32[]{:S(2)}) copy-start(f32[16,8,128]{2,1,0:T(8,128)} %v_ref.3) | copy-start | bytes 196612
  6.1 7.8 %copy-start.4 = (f32[15,8,128]{2,1,0:T(8,128)S(1)}, f32[15,8,128]{2,1,0:T(8,128)}, u32[]{:S(2)}) copy-start(f32[15,8,128]{2,1,0:T(8,128)} %mix_ref.1) | copy-start | bytes 184324
  6.1 5.8 %collective-permute-start.36 = (f32[112,128]{1,0:T(8,128)S(1)}, f32[112,128]{1,0:T(8,128)S(1)}, u32[]{:S(2)}, u32[]{:S(2)}) collective-permute-start(f32[112,128]{1,0:T(8,128)S(1)} %get-tuple-element.223.own_ref), channel_id=1, source_target_pairs={{1,11},{3,9},{5,7},{7,5},{9,3},{11,1},{13,31},{15,29},{17,27},{19,... | collective-permute-start | bytes 172040 | tf_op jit(solution)/shard_map/cond/branch_10_fun/ppermute | solution.py:539
  7.8 6.0 %collective-permute-start.35 = (f32[104,128]{1,0:T(8,128)S(1)}, f32[104,128]{1,0:T(8,128)S(1)}, u32[]{:S(2)}, u32[]{:S(2)}) collective-permute-start(f32[104,128]{1,0:T(8,128)S(1)} %get-tuple-element.222), channel_id=1, source_target_pairs={{2,0},{4,2},{6,4},{8,6},{10,8},{12,10},{14,12},{16,14},{18,16},{20... | collective-permute-start | bytes 159752 | tf_op jit(solution)/shard_map/cond/branch_10_fun/ppermute | solution.py:546
  12.0 1.8 %collective-permute-start.37 = (f32[16,128]{1,0:T(8,128)S(1)}, f32[16,128]{1,0:T(8,128)S(1)}, u32[]{:S(2)}, u32[]{:S(2)}) collective-permute-start(f32[16,128]{1,0:T(8,128)S(1)} %slice.106), channel_id=1, source_target_pairs={{0,1},{1,0},{2,3},{3,2},{4,5},{5,4},{6,7},{7,6},{8,9},{9,8},{10,11... | collective-permute-start | bytes 24584 | tf_op jit(solution)/shard_map/cond/branch_10_fun/ppermute | solution.py:540
